TPU v7x, 32 devices: a whole 2x2x4 slice. The times are simulated.
32 devices in a mesh: gx: 8 (over z, y), gy: 4 (over x, core).
Axes of the slice: x: 2, y: 2, z: 4, core: 2. Of those that a mesh axis runs over, the one named last changes fastest.
Arguments:
- mass_per_volume: float32 [64, 512, 32], P('gx', 'gy'), may hold values from 0.5 to 2
- momentum: float32 [3, 64, 512, 32], P(None, 'gx', 'gy'), may hold values from -0.9 to 0.9
- energy: float32 [64, 512, 32], P('gx', 'gy'), may hold values from 3 to 8
Outputs:
- tendency: float32 [5, 64, 512, 32], P(None, 'gx', 'gy')
- advanced: float32 [5, 64, 512, 32], P(None, 'gx', 'gy')
All inputs are finite; a program needn't handle non-finite values.
Results may differ from a plain program's by a relative error of at most 0.00016.
Values sent between devices are 32-bit elements; how exact they have to be, the bound alone decides.
No kernel may reach another device: no remote copies, remote signals or barrier semaphores. Data moves between devices by JAX's collectives and lax.ppermute only.
A program may use at most 64 MiB of HBM per device.

v0:
```python
import jax
import jax.numpy as jnp
import numpy as np
from jax import lax
from jax.sharding import PartitionSpec as P

CX = 8
CY = 8
NZ = 512
HALO = 4


heat_ratio = 1.4
shear_resistance_reference = 0.08
sutherland_power_law = 0.7
prandtl = 0.72
section_step = 0.05
compact_alpha = 1.0 / 3.0
compact_near = 14.0 / 9.0
compact_far = 1.0 / 9.0


def padded(array, sides, width):
    for axis, dim in sides:
        devices, length = (lax.axis_size(axis), array.shape[dim])
        up = [(i, (i + 1) % devices) for i in range(devices)]
        down = [(j, i) for i, j in up]
        last = lax.slice_in_dim(array, length - width, length, axis=dim)
        initial = lax.slice_in_dim(array, 0, width, axis=dim)
        before = lax.ppermute(last, axis, up)
        after = lax.ppermute(initial, axis, down)
        array = jnp.concatenate([before, array, after], axis=dim)
    return array


def tridiagonal_inverse_product(length, stencil):
    solved = np.array(stencil)
    upper_ratio = np.zeros(length)
    for row_index in range(length):
        if row_index == 0:
            pivot_value = 1.0
            solved[row_index] = solved[row_index] / pivot_value
        else:
            pivot_value = 1.0 - compact_alpha * upper_ratio[row_index - 1]
            solved[row_index] = (
                solved[row_index] - compact_alpha * solved[row_index - 1]
            ) / pivot_value
        upper_ratio[row_index] = compact_alpha / pivot_value
    for row_index in range(length - 2, -1, -1):
        solved[row_index] = solved[row_index] - upper_ratio[row_index] * solved[row_index + 1]
    return solved


def compact_matrix(block_size, margin):
    length = block_size + 2 * margin
    stencil = compact_near / 2.0 * (np.eye(length, k=1) - np.eye(length, k=-1))
    stencil = stencil + compact_far / 4.0 * (np.eye(length, k=2) - np.eye(length, k=-2))
    inverse_product = tridiagonal_inverse_product(length, stencil)
    return inverse_product[margin : margin + block_size].astype(np.float32)


def pitch_matrix(total, block_size):
    matrix = compact_matrix(block_size, HALO)
    result = np.zeros((total, total), np.float32)
    rows_all = np.arange(total)
    block_start = rows_all // block_size * block_size
    for offset in range(block_size + 2 * HALO):
        columns = (block_start - HALO + offset) % total
        result[rows_all, columns] += matrix[rows_all % block_size, offset]
    return result


def span_matrix(total):
    offsets = np.arange(total)[:, None] - np.arange(total)[None, :]
    angles = np.pi * offsets / total
    signs = np.where(offsets % 2 == 0, 1.0, -1.0)
    sines = np.where(offsets == 0, 1.0, np.sin(angles))
    result = np.where(offsets == 0, 0.0, np.pi / total * signs * np.cos(angles) / sines)
    return result.astype(np.float32)


def right_side(conserved, gradients_of, derive_x, derive_y, derive_z):
    mass_per_volume = conserved[0]
    momentum = conserved[1:4]
    energy = conserved[4]
    local_speed_vector = momentum / mass_per_volume
    kinetic = 0.5 * jnp.sum(momentum * local_speed_vector, axis=0)
    normal_force_per_area = (heat_ratio - 1.0) * (energy - kinetic)
    thermal_state = normal_force_per_area / mass_per_volume
    basic_quantities = jnp.concatenate([local_speed_vector, thermal_state[None]], 0)
    gradients = gradients_of(basic_quantities)
    shear_resistance = shear_resistance_reference * jnp.power(thermal_state, sutherland_power_law)
    conductivity = shear_resistance * heat_ratio / ((heat_ratio - 1.0) * prandtl)
    dilatation = gradients[0][0] + gradients[1][1] + gradients[2][2]
    derivers = (derive_x, derive_y, derive_z)
    accumulated = None
    for direction in range(3):
        stress_column = [
            shear_resistance * (gradients[direction][component] + gradients[component][direction])
            for component in range(3)
        ]
        stress_column[direction] = (
            stress_column[direction] - 2.0 / 3.0 * shear_resistance * dilatation
        )
        fluxes = [momentum[direction]]
        for component in range(3):
            moment_flux = (
                momentum[component] * local_speed_vector[direction] - stress_column[component]
            )
            if component == direction:
                moment_flux = moment_flux + normal_force_per_area
            fluxes.append(moment_flux)
        work_term = (
            stress_column[0] * local_speed_vector[0]
            + stress_column[1] * local_speed_vector[1]
            + stress_column[2] * local_speed_vector[2]
        )
        fluxes.append(
            (energy + normal_force_per_area) * local_speed_vector[direction]
            - work_term
            - conductivity * gradients[direction][3]
        )
        divergence_part = derivers[direction](jnp.stack(fluxes))
        accumulated = divergence_part if accumulated is None else accumulated + divergence_part
    return -accumulated


def per_device(mass_per_volume, momentum, energy):
    conserved = jnp.concatenate([mass_per_volume[None], momentum, energy[None]], 0)
    highest = lax.Precision.HIGHEST
    x_matrix = jnp.asarray(compact_matrix(CX, HALO))
    z_matrix = jnp.asarray(span_matrix(NZ))

    def apply_x(extended):
        return jnp.einsum("il,flab->fiab", x_matrix, extended, precision=highest)

    def flux_x(values):
        return apply_x(padded(values, (("gx", 1),), HALO))

    y_matrix = jnp.asarray(pitch_matrix(conserved.shape[3], CY))

    def apply_y(values):
        return jnp.einsum("fabk,jk->fabj", values, y_matrix, precision=highest)

    def derive_span(values):
        lines = jnp.transpose(
            lax.all_to_all(values, "gy", split_axis=3, concat_axis=2, tiled=True), (0, 1, 3, 2)
        )
        derived = jnp.einsum("fack,jk->facj", lines, z_matrix, precision=highest)
        returned = lax.all_to_all(derived, "gy", split_axis=3, concat_axis=2, tiled=True)
        return jnp.transpose(returned, (0, 1, 3, 2))

    def gradients_of(basic_quantities):
        extended = padded(basic_quantities, (("gx", 1),), HALO)
        return (apply_x(extended), apply_y(basic_quantities), derive_span(basic_quantities))

    tendency = right_side(conserved, gradients_of, flux_x, apply_y, derive_span)
    advanced = conserved + section_step * tendency
    return (tendency, advanced)


def solution(mesh):
    in_specs = (P("gx", "gy", None), P(None, "gx", "gy", None), P("gx", "gy", None))
    out_specs = (P(None, "gx", "gy", None), P(None, "gx", "gy", None))
    return jax.shard_map(
        per_device, mesh=mesh, in_specs=in_specs, out_specs=out_specs, check_vma=False
    )
```

profile of v0, /device:TPU:0, one launch (start us, length us, event | category | flops | bytes accessed | tf_op | source)
XLA Modules:
  0.0 135.4 jit_solution(3081403509513194817)
XLA Ops:
  0.6 1.0 copy.34
  1.7 1.3 broadcast_divide_fusion
  4.8 4.3 %all-to-all-start = ((f32[4,8,128,32]{2,1,0,3:T(8,128)}), f32[4,8,128,32]{2,1,0,3:T(8,128)S(1)}, u32[]{:S(2)}, u32[]{:S(2)}) async-start(f32[4,8,128,32]{2,1,0,3:T(8,128)} %copy.41), calls=%async_computation | async-start | bytes 1048576 | tf_op jit(solution)/shard_map/all_to_all | solution.py:147
  10.1 2.2 %collective-permute-start = (f32[4,4,128,32]{2,1,3,0:T(4,128)}, f32[4,4,128,32]{2,1,3,0:T(4,128)}, u32[]{:S(2)}, u32[]{:S(2)}) collective-permute-start(f32[4,4,128,32]{2,1,3,0:T(4,128)} %get-tuple-element.26), channel_id=1, source_target_pairs={{0,4},{4,8},{8,12},{12,16},{16,20},{20,24},{24,28},{28,0},{1,5},{5... | collective-permute-start | bytes 786440 | tf_op jit(solution)/shard_map/ppermute | solution.py:30
  12.3 3.0 %collective-permute-start.1 = (f32[4,4,128,32]{2,1,3,0:T(4,128)}, f32[4,4,128,32]{2,1,3,0:T(4,128)}, u32[]{:S(2)}, u32[]{:S(2)}) collective-permute-start(f32[4,4,128,32]{2,1,3,0:T(4,128)} %get-tuple-element.27), channel_id=1, source_target_pairs={{4,0},{8,4},{12,8},{16,12},{20,16},{24,20},{28,24},{0,28},{5,1},{9... | collective-permute-start | bytes 786440 | tf_op jit(solution)/shard_map/ppermute | solution.py:31
  18.0 1.3 fusion.30
  19.3 7.5 %copy.43 = f32[4,8,8,512]{2,1,0,3:T(8,128)} copy(f32[4,8,8,512]{3,2,1,0:T(8,128)S(1)} %fusion.30) | data formatting | bytes 1048576 | tf_op jit(solution)/shard_map/fack,jk->facj/dot_general | solution.py:149
  26.8 7.3 %reshape.16 = f32[4,1,32768]{2,1,0:T(1,128)} reshape(f32[512,4,8,8]{3,2,1,0:T(8,128)} %bitcast.262) | data formatting | bytes 1048576
  34.1 3.7 %all-to-all-start.1 = ((f32[4,1,32768]{2,1,0:T(1,128)}), f32[4,1,32768]{2,1,0:T(1,128)S(1)}, u32[]{:S(2)}, u32[]{:S(2)}) async-start(f32[4,1,32768]{2,1,0:T(1,128)} %reshape.16), calls=%async_computation.1 | async-start | bytes 1048576 | tf_op jit(solution)/shard_map/all_to_all | solution.py:150
  37.8 1.9 %convolution_bitcast_fusion = f32[4,8,128,32]{2,1,3,0:T(8,128)S(1)} fusion(f32[8,16,1,1]{1,0,3,2:T(8,128)S(1)} %copy-done.14, f32[4,4,128,32]{2,1,3,0:T(4,128)} %collective-permute-done.1, f32[1,8,128,32]{2,1,3,0:T(8,128)S(1)} %bitcast.266, f32[3,8,128,32]{2,1,3,0:T(8,128)S(1)} %get-tuple-element.28, f32[4,4,128,32]{2,1,3,0:T(4,128)} %collective-permute-done), kind=kOutput, calls=%fused_computation.10 | convolution fusion | flops 25952256 | bytes 1573376 | tf_op jit(solution)/shard_map/il,flab->fiab/dot_general | solution.py:135
  40.5 5.9 %all-to-all-done.1 = f32[4,1,32768]{2,1,0:T(1,128)S(1)} async-done(((f32[4,1,32768]{2,1,0:T(1,128)}), f32[4,1,32768]{2,1,0:T(1,128)S(1)}, u32[]{:S(2)}, u32[]{:S(2)}) %all-to-all-start.1) | async-done | bytes 524320 | tf_op jit(solution)/shard_map/all_to_all | solution.py:150
  47.0 2.2 %reduce = f32[4,32768]{1,0:T(4,128)S(1)} reduce(f32[4,1,32768]{2,1,0:T(1,128)S(1)} %all-to-all-done.1, f32[]{:T(128)} %broadcast.6), dimensions={1}, to_apply=%all_to_all.56.reduce_sub_computation | reduce | bytes 1048580 | tf_op jit(solution)/shard_map/all_to_all | solution.py:150
  49.2 8.0 %reshape.17 = f32[512,4,8,8]{3,2,1,0:T(8,128)} reshape(f32[4,32768]{1,0:T(4,128)S(1)} %reduce) | data formatting | bytes 1048576
  57.2 5.1 %copy.44 = f32[4,8,8,4,128]{4,1,2,3,0:T(8,128)S(1)} copy(f32[4,8,8,4,128]{2,1,0,4,3:T(8,128)} %bitcast.263) | data formatting | bytes 1048576 | tf_op jit(solution)/shard_map/all_to_all | solution.py:150
  62.3 1.8 %bitcast_dynamic-update-slice_fusion.4 = (f32[5,8,128,32]{2,1,3,0:T(8,128)}, f32[8,128,32]{1,0,2:T(8,128)S(1)}, f32[5,8,128,32]{2,1,3,0:T(8,128)S(1)}) fusion(f32[5,8,128,32]{2,1,3,0:T(8,128)} %get-tuple-element.10, f32[8,128,32]{1,0,2:T(8,128)S(1)} %get-tuple-element.15, f32[3,8,128,32]{2,1,3,0:T(8,128)S(1)} %get-tuple-element.32, ...), kind=kLoop, calls=%fused_computation.71 | loop fusion | flops 360447 | bytes 1441792
  66.8 4.3 %all-to-all-start.2 = ((f32[5,8,128,32]{2,1,0,3:T(8,128)}), f32[5,8,128,32]{2,1,0,3:T(8,128)}, u32[]{:S(2)}, u32[]{:S(2)}) async-start(f32[5,8,128,32]{2,1,0,3:T(8,128)} %copy.53), calls=%async_computation.2 | async-start | bytes 1310720 | tf_op jit(solution)/shard_map/all_to_all | solution.py:147
  71.2 2.0 %fusion.54 = (f32[5,8,128,32]{2,1,3,0:T(8,128)}, f32[5,8,128,32]{2,1,3,0:T(8,128)S(1)}) fusion(f32[5,8,128,32]{2,1,3,0:T(8,128)} %get-tuple-element.6, f32[1,8,128,32]{2,3,1,0:T(8,128)} %get-tuple-element.22, f32[8,128,32]{1,0,2:T(8,128)S(1)} %get-tuple-element.7, f32[8,128,32]{1,0,2:T(8,128)S(1)} %get-tuple-element.11, ...), kind=kLoop, calls=%fused_computation.64 | loop fusion | flops 884736 | bytes 2097152 | tf_op jit(solution)/shard_map/stack | solution.py:123
  73.2 8.3 %all-to-all-done.2 = f32[5,8,128,32]{2,1,0,3:T(8,128)} async-done(((f32[5,8,128,32]{2,1,0,3:T(8,128)}), f32[5,8,128,32]{2,1,0,3:T(8,128)}, u32[]{:S(2)}, u32[]{:S(2)}) %all-to-all-start.2) | async-done | bytes 655392 | tf_op jit(solution)/shard_map/all_to_all | solution.py:147
  81.5 2.4 %fusion.25 = f32[5,8,8,512]{3,2,1,0:T(8,128)S(1)} fusion(f32[512,512,1,1]{1,0,3,2:T(8,128)S(1)} %copy-done, f32[5,8,128,4,8]{2,1,0,4,3:T(8,128)} %bitcast.48), kind=kOutput, calls=%fused_computation.22 | convolution fusion | flops 1006632960 | bytes 2359296 | tf_op jit(solution)/shard_map/fack,jk->facj/dot_general | solution.py:149
  83.8 5.5 %copy.55 = f32[5,8,8,512]{2,1,0,3:T(8,128)} copy(f32[5,8,8,512]{3,2,1,0:T(8,128)S(1)} %fusion.25) | data formatting | bytes 1310720 | tf_op jit(solution)/shard_map/fack,jk->facj/dot_general | solution.py:149
  89.3 8.4 %reshape.18 = f32[4,1,40960]{2,1,0:T(1,128)} reshape(f32[512,5,8,8]{3,2,1,0:T(8,128)} %bitcast.260) | data formatting | bytes 1310720
  97.7 3.5 %all-to-all-start.3 = ((f32[4,1,40960]{2,1,0:T(1,128)}), f32[4,1,40960]{2,1,0:T(1,128)S(1)}, u32[]{:S(2)}, u32[]{:S(2)}) async-start(f32[4,1,40960]{2,1,0:T(1,128)} %reshape.18), calls=%async_computation.3 | async-start | bytes 1310720 | tf_op jit(solution)/shard_map/all_to_all | solution.py:150
  102.0 2.2 %collective-permute-start.2 = (f32[5,4,128,32]{2,1,3,0:T(4,128)}, f32[5,4,128,32]{2,1,3,0:T(4,128)}, u32[]{:S(2)}, u32[]{:S(2)}) collective-permute-start(f32[5,4,128,32]{2,1,3,0:T(4,128)} %get-tuple-element.20), channel_id=1, source_target_pairs={{0,4},{4,8},{8,12},{12,16},{16,20},{20,24},{24,28},{28,0},{1,5},{5... | collective-permute-start | bytes 983048 | tf_op jit(solution)/shard_map/ppermute | solution.py:30
  104.2 3.0 %collective-permute-start.3 = (f32[5,4,128,32]{2,1,3,0:T(4,128)S(1)}, f32[5,4,128,32]{2,1,3,0:T(4,128)}, u32[]{:S(2)}, u32[]{:S(2)}) collective-permute-start(f32[5,4,128,32]{2,1,3,0:T(4,128)S(1)} %get-tuple-element.21), channel_id=1, source_target_pairs={{4,0},{8,4},{12,8},{16,12},{20,16},{24,20},{28,24},{0,28},{5,1},{9... | collective-permute-start | bytes 983048 | tf_op jit(solution)/shard_map/ppermute | solution.py:31
  107.3 2.7 %fusion.28 = f32[5,8,128,32]{2,3,1,0:T(8,128)} fusion(f32[32,32,1,1]{1,0,3,2:T(8,128)S(1)} %copy-done.13, f32[5,8,128,32]{2,1,3,0:T(8,128)} %get-tuple-element.18), kind=kOutput, calls=%fused_computation.25 | convolution fusion | flops 62914560 | bytes 1314816 | tf_op jit(solution)/shard_map/fabk,jk->fabj/dot_general | solution.py:143
  109.9 1.5 %all-to-all-done.3 = f32[4,1,40960]{2,1,0:T(1,128)S(1)} async-done(((f32[4,1,40960]{2,1,0:T(1,128)}), f32[4,1,40960]{2,1,0:T(1,128)S(1)}, u32[]{:S(2)}, u32[]{:S(2)}) %all-to-all-start.3) | async-done | bytes 655392 | tf_op jit(solution)/shard_map/all_to_all | solution.py:150
  111.4 2.6 %reduce.1 = f32[4,40960]{1,0:T(4,128)S(1)} reduce(f32[4,1,40960]{2,1,0:T(1,128)S(1)} %all-to-all-done.3, f32[]{:T(128)} %broadcast.6), dimensions={1}, to_apply=%all_to_all.64.reduce_sub_computation | reduce | bytes 1310724 | tf_op jit(solution)/shard_map/all_to_all | solution.py:150
  114.0 9.9 %reshape.19 = f32[512,5,8,8]{3,2,1,0:T(8,128)} reshape(f32[4,40960]{1,0:T(4,128)S(1)} %reduce.1) | data formatting | bytes 1310720
  123.9 6.7 %copy.56 = f32[5,8,8,4,128]{4,1,2,3,0:T(8,128)} copy(f32[5,8,8,4,128]{2,1,0,4,3:T(8,128)} %bitcast.261) | data formatting | bytes 1310720 | tf_op jit(solution)/shard_map/all_to_all | solution.py:150
  130.6 2.9 %maximum_add_fusion = (f32[5,8,128,32]{2,1,3,0:T(8,128)S(1)}, f32[5,8,128,32]{2,1,3,0:T(8,128)S(1)}) fusion(f32[1,8,128,32]{2,1,3,0:T(8,128)S(1)} %copy-done.12, f32[3,8,128,32]{2,1,3,0:T(8,128)S(1)} %get-tuple-element.32, f32[1,8,128,32]{2,1,3,0:T(8,128)S(1)} %copy-done.11, f32[5,8,128,32]{2,1,3,0:T(8,128)} %bitcast.271, f32[5,8,128,32]{2,3,1,0:T(8,128)} %fusion.28, ...), kind=kOutput, calls=%fused_computation.21 | convolution fusion | flops 33259520 | bytes 4588032 | tf_op jit(solution)/shard_map/il,flab->fiab/dot_general | solution.py:135
  133.4 1.0 copy.61
  134.4 1.0 copy.60
  (55 shorter events, 10.3 us)
Async XLA Ops:
  0.6 2.3 %copy-start.8 = (f32[8,128,32]{1,2,0:T(8,128)S(1)}, f32[8,128,32]{1,2,0:T(8,128)}, u32[]{:S(2)}) copy-start(f32[8,128,32]{1,2,0:T(8,128)} %param.6) | copy-start | bytes 393220
  0.6 2.3 %copy-start.3 = (f32[8,128,32]{1,2,0:T(8,128)S(1)}, f32[8,128,32]{1,2,0:T(8,128)}, u32[]{:S(2)}) copy-start(f32[8,128,32]{1,2,0:T(8,128)} %param.8) | copy-start | bytes 393220
  4.8 10.6 %copy-start.13 = (f32[32,32,1,1]{1,0,3,2:T(8,128)S(1)}, f32[32,32,1,1]{1,0,3,2:T(8,128)}, u32[]{:S(2)}) copy-start(f32[32,32,1,1]{1,0,3,2:T(8,128)} %constant.31) | copy-start | bytes 12292
  4.8 13.2 %all-to-all-start = ((f32[4,8,128,32]{2,1,0,3:T(8,128)}), f32[4,8,128,32]{2,1,0,3:T(8,128)S(1)}, u32[]{:S(2)}, u32[]{:S(2)}) async-start(f32[4,8,128,32]{2,1,0,3:T(8,128)} %copy.41), calls=%async_computation | async-start | bytes 1048576 | tf_op jit(solution)/shard_map/all_to_all | solution.py:147
  10.1 7.9 %copy-start = (f32[512,512,1,1]{1,0,3,2:T(8,128)S(1)}, f32[512,512,1,1]{1,0,3,2:T(8,128)}, u32[]{:S(2)}) copy-start(f32[512,512,1,1]{1,0,3,2:T(8,128)} %constant.32) | copy-start | bytes 3145732
  10.1 27.7 %collective-permute-start = (f32[4,4,128,32]{2,1,3,0:T(4,128)}, f32[4,4,128,32]{2,1,3,0:T(4,128)}, u32[]{:S(2)}, u32[]{:S(2)}) collective-permute-start(f32[4,4,128,32]{2,1,3,0:T(4,128)} %get-tuple-element.26), channel_id=1, source_target_pairs={{0,4},{4,8},{8,12},{12,16},{16,20},{20,24},{24,28},{28,0},{1,5},{5... | collective-permute-start | bytes 786440 | tf_op jit(solution)/shard_map/ppermute | solution.py:30
  12.3 25.5 %collective-permute-start.1 = (f32[4,4,128,32]{2,1,3,0:T(4,128)}, f32[4,4,128,32]{2,1,3,0:T(4,128)}, u32[]{:S(2)}, u32[]{:S(2)}) collective-permute-start(f32[4,4,128,32]{2,1,3,0:T(4,128)} %get-tuple-element.27), channel_id=1, source_target_pairs={{4,0},{8,4},{12,8},{16,12},{20,16},{24,20},{28,24},{0,28},{5,1},{9... | collective-permute-start | bytes 786440 | tf_op jit(solution)/shard_map/ppermute | solution.py:31
  17.4 44.9 %copy-start.6 = (f32[1,8,128,32]{2,3,1,0:T(8,128)}, f32[1,8,128,32]{2,3,1,0:T(8,128)S(1)}, u32[]{:S(2)}) copy-start(f32[1,8,128,32]{2,3,1,0:T(8,128)S(1)} %get-tuple-element.25) | copy-start | bytes 393220
  26.8 11.0 %copy-start.14 = (f32[8,16,1,1]{1,0,3,2:T(8,128)S(1)}, f32[8,16,1,1]{1,0,3,2:T(8,128)}, u32[]{:S(2)}) copy-start(f32[8,16,1,1]{1,0,3,2:T(8,128)} %constant.30) | copy-start | bytes 1540
  34.1 12.3 %all-to-all-start.1 = ((f32[4,1,32768]{2,1,0:T(1,128)}), f32[4,1,32768]{2,1,0:T(1,128)S(1)}, u32[]{:S(2)}, u32[]{:S(2)}) async-start(f32[4,1,32768]{2,1,0:T(1,128)} %reshape.16), calls=%async_computation.1 | async-start | bytes 1048576 | tf_op jit(solution)/shard_map/all_to_all | solution.py:150
  37.7 2.0 %copy-start.9 = (f32[1,8,128,32]{2,3,1,0:T(8,128)S(1)}, f32[1,8,128,32]{2,3,1,0:T(8,128)}, u32[]{:S(2)}) copy-start(f32[1,8,128,32]{2,3,1,0:T(8,128)} %get-tuple-element.24) | copy-start | bytes 393220
  39.7 6.7 %copy-start.4 = (f32[4,8,128,32]{2,1,3,0:T(8,128)}, f32[4,8,128,32]{2,1,3,0:T(8,128)S(1)}, u32[]{:S(2)}) copy-start(f32[4,8,128,32]{2,1,3,0:T(8,128)S(1)} %convolution_bitcast_fusion) | copy-start | bytes 1572868
  62.3 1.8 %copy-start.5 = (f32[4,8,128,32]{2,1,3,0:T(8,128)S(1)}, f32[4,8,128,32]{2,1,3,0:T(8,128)}, u32[]{:S(2)}) copy-start(f32[4,8,128,32]{2,1,3,0:T(8,128)} %copy-done.4) | copy-start | bytes 1572868
  62.3 1.9 %copy-start.10 = (f32[1,8,128,32]{2,3,1,0:T(8,128)S(1)}, f32[1,8,128,32]{2,3,1,0:T(8,128)}, u32[]{:S(2)}) copy-start(f32[1,8,128,32]{2,3,1,0:T(8,128)} %get-tuple-element.23) | copy-start | bytes 393220
  65.1 0.9 copy-start.1
  65.9 5.2 %copy-start.7 = (f32[1,8,128,32]{2,3,1,0:T(8,128)S(1)}, f32[1,8,128,32]{2,3,1,0:T(8,128)}, u32[]{:S(2)}) copy-start(f32[1,8,128,32]{2,3,1,0:T(8,128)} %copy-done.6) | copy-start | bytes 393220
  66.8 4.3 %copy-start.2 = (f32[5,8,128,32]{2,1,3,0:T(8,128)S(1)}, f32[5,8,128,32]{2,1,3,0:T(8,128)}, u32[]{:S(2)}) copy-start(f32[5,8,128,32]{2,1,3,0:T(8,128)} %copy-done.1) | copy-start | bytes 1966084
  66.8 14.6 %all-to-all-start.2 = ((f32[5,8,128,32]{2,1,0,3:T(8,128)}), f32[5,8,128,32]{2,1,0,3:T(8,128)}, u32[]{:S(2)}, u32[]{:S(2)}) async-start(f32[5,8,128,32]{2,1,0,3:T(8,128)} %copy.53), calls=%async_computation.2 | async-start | bytes 1310720 | tf_op jit(solution)/shard_map/all_to_all | solution.py:147
  97.7 13.7 %all-to-all-start.3 = ((f32[4,1,40960]{2,1,0:T(1,128)}), f32[4,1,40960]{2,1,0:T(1,128)S(1)}, u32[]{:S(2)}, u32[]{:S(2)}) async-start(f32[4,1,40960]{2,1,0:T(1,128)} %reshape.18), calls=%async_computation.3 | async-start | bytes 1310720 | tf_op jit(solution)/shard_map/all_to_all | solution.py:150
  102.0 28.5 %collective-permute-start.2 = (f32[5,4,128,32]{2,1,3,0:T(4,128)}, f32[5,4,128,32]{2,1,3,0:T(4,128)}, u32[]{:S(2)}, u32[]{:S(2)}) collective-permute-start(f32[5,4,128,32]{2,1,3,0:T(4,128)} %get-tuple-element.20), channel_id=1, source_target_pairs={{0,4},{4,8},{8,12},{12,16},{16,20},{20,24},{24,28},{28,0},{1,5},{5... | collective-permute-start | bytes 983048 | tf_op jit(solution)/shard_map/ppermute | solution.py:30
  104.2 26.3 %collective-permute-start.3 = (f32[5,4,128,32]{2,1,3,0:T(4,128)S(1)}, f32[5,4,128,32]{2,1,3,0:T(4,128)}, u32[]{:S(2)}, u32[]{:S(2)}) collective-permute-start(f32[5,4,128,32]{2,1,3,0:T(4,128)S(1)} %get-tuple-element.21), channel_id=1, source_target_pairs={{4,0},{8,4},{12,8},{16,12},{20,16},{24,20},{28,24},{0,28},{5,1},{9... | collective-permute-start | bytes 983048 | tf_op jit(solution)/shard_map/ppermute | solution.py:31
  123.9 6.7 %copy-start.11 = (f32[1,8,128,32]{2,1,3,0:T(8,128)S(1)}, f32[1,8,128,32]{2,1,3,0:T(8,128)}, u32[]{:S(2)}) copy-start(f32[1,8,128,32]{2,1,3,0:T(8,128)} %get-tuple-element.33) | copy-start | bytes 393220
  123.9 6.7 %copy-start.12 = (f32[1,8,128,32]{2,1,3,0:T(8,128)S(1)}, f32[1,8,128,32]{2,1,3,0:T(8,128)}, u32[]{:S(2)}) copy-start(f32[1,8,128,32]{2,1,3,0:T(8,128)} %get-tuple-element.34) | copy-start | bytes 393220
  123.9 6.7 %copy-start.15 = (f32[8,16,1,1]{1,0,3,2:T(8,128)S(1)}, f32[8,16,1,1]{1,0,3,2:T(8,128)}, u32[]{:S(2)}) copy-start(f32[8,16,1,1]{1,0,3,2:T(8,128)} %constant.30) | copy-start | bytes 1540
where the time goes:
time: 136 us; the launch traced here: 135 us
  local copies, waits for them, and re-layouts  66.5 us (49%)
  starting transfers between devices  26.3 us (19%)
  waiting for transfers between devices  16.2 us (12%)
  other arithmetic  13.7 us (10%)
  matrix products  11.8 us (9%)
    unnamed x40, local copies, waits for them, and re-layouts  37.8 us
    dot_general x2, local copies, waits for them, and re-layouts, derive_span(): derived = jnp.einsum('fack,jk->facj', lines, z_matrix, precision=highest)  12.9 us
    all_to_all x3, local copies, waits for them, and re-layouts, derive_span(): lax.all_to_all(derived, 'gy', split_axis=3, concat_axis=2, tiled=True)  12.4 us
    all_to_all x2, waiting for transfers between devices, derive_span(): lax.all_to_all(values, 'gy', split_axis=3, concat_axis=2, tiled=True)  8.83 us
    all_to_all x2, starting transfers between devices, derive_span(): lax.all_to_all(values, 'gy', split_axis=3, concat_axis=2, tiled=True)  8.64 us
    all_to_all x2, waiting for transfers between devices, derive_span(): lax.all_to_all(derived, 'gy', split_axis=3, concat_axis=2, tiled=True)  7.35 us
    all_to_all x2, starting transfers between devices, derive_span(): lax.all_to_all(derived, 'gy', split_axis=3, concat_axis=2, tiled=True)  7.14 us
    ppermute x2, starting transfers between devices, padded(): after = lax.ppermute(initial, axis, down)  6.07 us
  transfers between devices with their start and end apart: 8, of which 4 were waited for; matrix products, arithmetic and copies ran while one was open for 34% of the time, Pallas kernels for 0%

commit v1 on v0

--- a/solution.py
+++ b/solution.py
@@ -1,7 +1,11 @@
+import functools
+
 import jax
 import jax.numpy as jnp
 import numpy as np
 from jax import lax
+from jax.experimental import pallas as pl
+from jax.experimental.pallas import tpu as pltpu
 from jax.sharding import PartitionSpec as P
 
 CX = 8
@@ -19,18 +23,8 @@
 compact_near = 14.0 / 9.0
 compact_far = 1.0 / 9.0
 
-
-def padded(array, sides, width):
-    for axis, dim in sides:
-        devices, length = (lax.axis_size(axis), array.shape[dim])
-        up = [(i, (i + 1) % devices) for i in range(devices)]
-        down = [(j, i) for i, j in up]
-        last = lax.slice_in_dim(array, length - width, length, axis=dim)
-        initial = lax.slice_in_dim(array, 0, width, axis=dim)
-        before = lax.ppermute(last, axis, up)
-        after = lax.ppermute(initial, axis, down)
-        array = jnp.concatenate([before, array, after], axis=dim)
-    return array
+conduction = heat_ratio / ((heat_ratio - 1.0) * prandtl)
+enthalpy = heat_ratio / (heat_ratio - 1.0)
 
 
 def tridiagonal_inverse_product(length, stencil):
@@ -77,6 +71,319 @@
     sines = np.where(offsets == 0, 1.0, np.sin(angles))
     result = np.where(offsets == 0, 0.0, np.pi / total * signs * np.cos(angles) / sines)
     return result.astype(np.float32)
+
+
+F32 = jnp.float32
+BF16 = jnp.bfloat16
+
+
+def halves(matrix):
+    high = matrix.astype(BF16)
+    low = (matrix - np.asarray(high, np.float32)).astype(BF16)
+    return jnp.asarray(high), jnp.asarray(low)
+
+
+def split(values):
+    high = values.astype(BF16)
+    low = (values - high.astype(F32)).astype(BF16)
+    return high, low
+
+
+def dot(a, b):
+    return jnp.dot(a, b, preferred_element_type=F32)
+
+
+def right_product(values, matrix_high, matrix_low):
+    high, low = split(values)
+    return dot(high, matrix_high) + dot(low, matrix_high) + dot(high, matrix_low)
+
+
+def left_product(matrix_high, matrix_low, values):
+    high, low = split(values)
+    return dot(matrix_high, high) + dot(matrix_high, low) + dot(matrix_low, high)
+
+
+def compact_x(planes):
+    matrix = compact_matrix(CX, HALO).astype(np.float64)
+    length = CX + 2 * HALO
+    half = length // 2
+    odd = [planes[l] - planes[length - 1 - l] for l in range(half)]
+    even = [planes[l] + planes[length - 1 - l] for l in range(half)]
+    result = [None] * CX
+    for i in range(CX // 2):
+        first = None
+        second = None
+        for l in range(half):
+            a = float(0.5 * (matrix[i, l] - matrix[i, length - 1 - l]))
+            b = float(0.5 * (matrix[i, l] + matrix[i, length - 1 - l]))
+            first = a * odd[l] if first is None else first + a * odd[l]
+            second = b * even[l] if second is None else second + b * even[l]
+        result[i] = first + second
+        result[CX - 1 - i] = first - second
+    return result
+
+
+def extended_planes(before, own, after, field, rows):
+    return (
+        [before[field, l, rows, :] for l in range(HALO)]
+        + [own[field, l, rows, :] for l in range(CX)]
+        + [after[field, l, rows, :] for l in range(HALO)]
+    )
+
+
+def kernel_primitives(rho, mom, energy, prim, low, high):
+    for x in range(CX):
+        density = rho[x]
+        inverse = 1.0 / density
+        u = mom[0, x] * inverse
+        v = mom[1, x] * inverse
+        w = mom[2, x] * inverse
+        kinetic = 0.5 * (mom[0, x] * u + mom[1, x] * v + mom[2, x] * w)
+        temperature = (heat_ratio - 1.0) * (energy[x] - kinetic) * inverse
+        target = (low, x) if x < HALO else (high, x - HALO)
+        for f, value in enumerate((u, v, w, temperature)):
+            prim[f, x] = value
+            target[0][f, target[1]] = value
+        prim[4, x] = density
+
+
+def kernel_local_gradients(prim, before, after, y_high, y_low, dx, dy, mu, shared):
+    rows_all = prim.shape[2]
+    for start in range(0, rows_all, 8):
+        rows = slice(start, start + 8)
+        for f in range(4):
+            derived = compact_x(extended_planes(before, prim, after, f, rows))
+            for x in range(CX):
+                dx[f, x, rows, :] = derived[x]
+    for x in range(CX):
+        viscosity = shear_resistance_reference * jnp.exp(
+            sutherland_power_law * jnp.log(prim[3, x])
+        )
+        mu[x] = viscosity
+        shared[0, x] = (2.0 / 3.0) * viscosity * dx[0, x]
+        shared[1, x] = viscosity * dx[2, x]
+    for f in range(4):
+        values = prim[f].reshape(-1, prim.shape[-1])
+        dy[f] = left_product(y_high[...], y_low[...], values).reshape(prim.shape[1:])
+
+
+def kernel_flux_x(me, prim, lines, dx, dy, mu, z_high, z_low, dz, flux, low, high):
+    count, _, _, rows, width = lines.shape
+    column = pl.ds(pl.multiple_of(me[0] * width, width), width)
+    for f in range(4):
+        values = jnp.concatenate(
+            [lines[s, f].reshape(-1, width) for s in range(count)], axis=1
+        )
+        dz[f] = right_product(values, z_high[:, column], z_low[:, column]).reshape(
+            prim.shape[1:]
+        )
+    for x in range(CX):
+        u, v, w, t, density = (prim[f, x] for f in range(5))
+        viscosity = mu[x]
+        dil = dx[0, x] + dy[1, x] + dz[2, x]
+        s1 = viscosity * (2.0 * dx[0, x] - (2.0 / 3.0) * dil)
+        s2 = viscosity * (dx[1, x] + dy[0, x])
+        s3 = viscosity * (dx[2, x] + dz[0, x])
+        m = density * u
+        pressure = density * t
+        total = m * (enthalpy * t + 0.5 * (u * u + v * v + w * w))
+        values = (
+            m,
+            m * u + pressure - s1,
+            m * v - s2,
+            m * w - s3,
+            total - (s1 * u + s2 * v + s3 * w) - conduction * viscosity * dx[3, x],
+        )
+        target = (low, x) if x < HALO else (high, x - HALO)
+        for f in range(5):
+            flux[f, x] = values[f]
+            target[0][f, target[1]] = values[f]
+
+
+def kernel_flux_yz(
+    me, prim, lines, dx, dy, dz, mu, y_high, y_low, z_high, z_low, part,
+    grad, dy_lines, flux, flux_y,
+):
+    count, _, _, rows, width = lines.shape
+    total_rows = CX * rows
+    column = pl.ds(pl.multiple_of(me[0] * width, width), width)
+    for f in range(4):
+        values = jnp.concatenate(
+            [lines[s, f].reshape(total_rows, width) for s in range(count)], axis=1
+        )
+        grad[f] = right_product(values, z_high[...], z_low[...])
+        if f in (1, 2):
+            dy_lines[f - 1] = left_product(y_high[...], y_low[...], values)
+
+    def flux_plane(x, carry):
+        at = pl.ds(pl.multiple_of(x * rows, rows), rows)
+        for s in range(count):
+            lanes = slice(s * width, (s + 1) * width)
+            u, v, w, t, density = (lines[s, f, x] for f in range(5))
+            viscosity = shear_resistance_reference * jnp.exp(
+                sutherland_power_law * jnp.log(t)
+            )
+            zu, zv, zw, zt = (grad[f, at, lanes] for f in range(4))
+            yv = dy_lines[0, at, lanes]
+            yw = dy_lines[1, at, lanes]
+            s1 = viscosity * zu
+            s2 = viscosity * (zv + yw)
+            s3 = viscosity * ((4.0 / 3.0) * zw - (2.0 / 3.0) * yv)
+            m = density * w
+            total = m * (enthalpy * t + 0.5 * (u * u + v * v + w * w))
+            flux[0, at, lanes] = m
+            flux[1, at, lanes] = m * u - s1
+            flux[2, at, lanes] = m * v - s2
+            flux[3, at, lanes] = m * w + density * t - s3
+            flux[4, at, lanes] = (
+                total - (s1 * u + s2 * v + s3 * w) - conduction * viscosity * zt
+            )
+        u, v, w, t, density = (prim[f, x] for f in range(5))
+        viscosity = mu[x]
+        dil = dx[0, x] + dy[1, x] + dz[2, x]
+        s1 = viscosity * (dy[0, x] + dx[1, x])
+        s2 = viscosity * (2.0 * dy[1, x] - (2.0 / 3.0) * dil)
+        s3 = viscosity * (dy[2, x] + dz[1, x])
+        m = density * v
+        total = m * (enthalpy * t + 0.5 * (u * u + v * v + w * w))
+        flux_y[0, at, :] = m
+        flux_y[1, at, :] = m * u - s1
+        flux_y[2, at, :] = m * v + density * t - s2
+        flux_y[3, at, :] = m * w - s3
+        flux_y[4, at, :] = (
+            total - (s1 * u + s2 * v + s3 * w) - conduction * viscosity * dy[3, x]
+        )
+        return carry
+
+    lax.fori_loop(0, CX, flux_plane, 0)
+    for f in range(5):
+        result = right_product(flux[f], z_high[:, column], z_low[:, column])
+        result = result + left_product(y_high[...], y_low[...], flux_y[f])
+        part[f] = result.reshape(prim.shape[1:])
+
+
+def kernel_finish(
+    me, rho, mom, energy, lines, shared, part, flux, before, after, z_high, z_low,
+    tendency, advanced, work,
+):
+    count, _, _, rows, width = lines.shape
+    total_rows = CX * rows
+    column = pl.ds(pl.multiple_of(me[0] * width, width), width)
+    for x in range(CX):
+        at = slice(x * rows, (x + 1) * rows)
+        for s in range(count):
+            lanes = slice(s * width, (s + 1) * width)
+            normal = shared[s, 0, x]
+            shear = shared[s, 1, x]
+            work[0, at, lanes] = -shear
+            work[1, at, lanes] = normal
+            work[2, at, lanes] = normal * lines[s, 2, x] - shear * lines[s, 0, x]
+    corrections = {}
+    for position, f in enumerate((1, 3, 4)):
+        corrections[f] = right_product(work[position], z_high[:, column], z_low[:, column])
+    for f in range(5):
+        total = part[f]
+        if f in corrections:
+            total = total + corrections[f].reshape(total.shape)
+        tendency[f] = total
+    for start in range(0, rows, 8):
+        chunk = slice(start, start + 8)
+        for f in range(5):
+            derived = compact_x(extended_planes(before, flux, after, f, chunk))
+            for x in range(CX):
+                value = -(tendency[f, x, chunk, :] + derived[x])
+                if f == 0:
+                    old = rho[x, chunk, :]
+                elif f == 4:
+                    old = energy[x, chunk, :]
+                else:
+                    old = mom[f - 1, x, chunk, :]
+                tendency[f, x, chunk, :] = value
+                advanced[f, x, chunk, :] = old + section_step * value
+
+
+def call(kernel, outputs, scratch, smem, cost, *operands):
+    in_specs = [pl.BlockSpec(memory_space=pltpu.VMEM) for _ in operands]
+    if smem:
+        in_specs[0] = pl.BlockSpec(memory_space=pltpu.SMEM)
+    return pl.pallas_call(
+        kernel,
+        out_shape=[jax.ShapeDtypeStruct(shape, F32) for shape in outputs],
+        in_specs=in_specs,
+        out_specs=[pl.BlockSpec(memory_space=pltpu.VMEM) for _ in outputs],
+        scratch_shapes=scratch,
+        cost_estimate=pl.CostEstimate(flops=cost, bytes_accessed=cost // 300, transcendentals=0),
+        compiler_params=pltpu.CompilerParams(vmem_limit_bytes=48 * 1024 * 1024),
+    )(*operands)
+
+
+def fast_device(mass_per_volume, momentum, energy):
+    rho = jnp.transpose(mass_per_volume, (0, 2, 1))
+    mom = jnp.transpose(momentum, (0, 1, 3, 2))
+    ene = jnp.transpose(energy, (0, 2, 1))
+    _, rows, width = rho.shape
+    count = lax.axis_size("gy")
+    length = count * width
+    me = lax.axis_index("gy").astype(jnp.int32).reshape(1)
+    z_high, z_low = halves(span_matrix(length).T)
+    y_high, y_low = halves(np.kron(np.eye(CX, dtype=np.float32), pitch_matrix(rows, CY)))
+    block = (CX, rows, width)
+    edge = (HALO, rows, width)
+    devices = lax.axis_size("gx")
+    up = [(i, (i + 1) % devices) for i in range(devices)]
+    down = [(j, i) for i, j in up]
+
+    prim, low, high = call(
+        kernel_primitives, [(5,) + block, (4,) + edge, (4,) + edge], [], False, 10**9,
+        rho, mom, ene,
+    )
+    lines = lax.all_gather(prim, "gy", axis=0, tiled=False)
+    before = lax.ppermute(high, "gx", up)
+    after = lax.ppermute(low, "gx", down)
+    dx, dy, mu, mine = call(
+        kernel_local_gradients, [(4,) + block, (4,) + block, block, (2,) + block], [],
+        False, 2 * 10**9, prim, before, after, y_high, y_low,
+    )
+    shared = lax.all_gather(mine, "gy", axis=0, tiled=False)
+    dz, flux, flux_low, flux_high = call(
+        kernel_flux_x, [(4,) + block, (5,) + block, (5,) + edge, (5,) + edge], [],
+        True, 2 * 10**9, me, prim, lines, dx, dy, mu, z_high, z_low,
+    )
+    flux_before = lax.ppermute(flux_high, "gx", up)
+    flux_after = lax.ppermute(flux_low, "gx", down)
+    (part,) = call(
+        kernel_flux_yz, [(5,) + block],
+        [
+            pltpu.VMEM((4, CX * rows, length), F32),
+            pltpu.VMEM((2, CX * rows, length), F32),
+            pltpu.VMEM((5, CX * rows, length), F32),
+            pltpu.VMEM((5, CX * rows, width), F32),
+        ],
+        True, 4 * 10**9, me, prim, lines, dx, dy, dz, mu, y_high, y_low, z_high, z_low,
+    )
+    tendency, advanced = call(
+        kernel_finish, [(5,) + block, (5,) + block],
+        [pltpu.VMEM((3, CX * rows, length), F32)],
+        True, 2 * 10**9, me, rho, mom, ene, lines, shared, part, flux, flux_before, flux_after,
+        z_high, z_low,
+    )
+    return (
+        jnp.transpose(tendency, (0, 1, 3, 2)),
+        jnp.transpose(advanced, (0, 1, 3, 2)),
+    )
+
+
+def padded(array, sides, width):
+    for axis, dim in sides:
+        devices, length = (lax.axis_size(axis), array.shape[dim])
+        up = [(i, (i + 1) % devices) for i in range(devices)]
+        down = [(j, i) for i, j in up]
+        last = lax.slice_in_dim(array, length - width, length, axis=dim)
+        initial = lax.slice_in_dim(array, 0, width, axis=dim)
+        before = lax.ppermute(last, axis, up)
+        after = lax.ppermute(initial, axis, down)
+        array = jnp.concatenate([before, array, after], axis=dim)
+    return array
 
 
 def right_side(conserved, gradients_of, derive_x, derive_y, derive_z):
@@ -125,7 +432,7 @@
     return -accumulated
 
 
-def per_device(mass_per_volume, momentum, energy):
+def plain_device(mass_per_volume, momentum, energy):
     conserved = jnp.concatenate([mass_per_volume[None], momentum, energy[None]], 0)
     highest = lax.Precision.HIGHEST
     x_matrix = jnp.asarray(compact_matrix(CX, HALO))
@@ -157,6 +464,13 @@
     tendency = right_side(conserved, gradients_of, flux_x, apply_y, derive_span)
     advanced = conserved + section_step * tendency
     return (tendency, advanced)
+
+
+def per_device(mass_per_volume, momentum, energy):
+    planes, width, rows = mass_per_volume.shape
+    if planes == CX and width % 128 == 0 and rows <= 32 and rows % CY == 0:
+        return fast_device(mass_per_volume, momentum, energy)
+    return plain_device(mass_per_volume, momentum, energy)
 
 
 def solution(mesh):

time: 136 us -> 76.1 us (0.56)
  local copies, waits for them, and re-layouts: 66.5 us -> 10 us
  Pallas kernels: 0 us -> 17.6 us
  starting transfers between devices: 26.3 us -> 11 us
  other arithmetic: 13.7 us -> 0 us
  between operations: 0.91 us -> 14.1 us
  matrix products: 11.8 us -> 0 us
  waiting for transfers between devices: 16.2 us -> 23 us
    unnamed x40 -> x38, local copies, waits for them, and re-layouts: 37.8 us -> 10 us
    pallas_call x0 -> x5, Pallas kernels: none -> 17.6 us  [call(): pl.pallas_call(kernel, out_shape=[jax.ShapeDtypeStruct(shape, F32) for sh...]
    all_to_all x4 -> x0, waiting for transfers between devices: 16.2 us -> none  [the longest x2 8.83 us: derive_span(): lax.all_to_all(values, 'gy', split_axis=3, concat_axis=2, tiled=True)]
    all_to_all x4 -> x0, starting transfers between devices: 15.8 us -> none  [the longest x2 8.64 us: derive_span(): lax.all_to_all(values, 'gy', split_axis=3, concat_axis=2, tiled=True)]
    ppermute x4, waiting for transfers between devices: 0.01 us -> 13.7 us  [the longest x1 8.03 us: fast_device(): before = lax.ppermute(high, 'gx', up)]
    dot_general x2 -> x0, local copies, waits for them, and re-layouts: 12.9 us -> none  [derive_span(): derived = jnp.einsum('fack,jk->facj', lines, z_matrix, precision=highest)]
    all_to_all x3 -> x0, local copies, waits for them, and re-layouts: 12.4 us -> none  [derive_span(): lax.all_to_all(derived, 'gy', split_axis=3, concat_axis=2, tiled=True)]
    dot_general x6 -> x0, matrix products: 11.8 us -> none  [the longest x2 4.76 us: apply_x(): return jnp.einsum('il,flab->fiab', x_matrix, extended, precision=highest)]
  transfers between devices with their start and end apart: 8 -> 6, of which waited for: 4 -> 5; matrix products, arithmetic and copies ran while one was open for 34% -> 0% of each run, Pallas kernels for 0% -> 17%
where the time goes in v1:
time: 76.1 us; the launch traced here: 75.6 us
  waiting for transfers between devices  23 us (30%)
  Pallas kernels  17.6 us (23%)
  between operations  14.1 us (19%)
  starting transfers between devices  11 us (14%)
  local copies, waits for them, and re-layouts  10 us (13%)
    pallas_call x5, Pallas kernels, call(): pl.pallas_call(kernel, out_shape=[jax.ShapeDtypeStruct(shape, F32) for sh...  17.6 us
    unnamed x38, local copies, waits for them, and re-layouts  10 us
    all_gather x1, waiting for transfers between devices, fast_device(): lines = lax.all_gather(prim, 'gy', axis=0, tiled=False)  9.24 us
    ppermute x1, waiting for transfers between devices, fast_device(): before = lax.ppermute(high, 'gx', up)  8.03 us
    ppermute x1, starting transfers between devices, fast_device(): flux_after = lax.ppermute(flux_low, 'gx', down)  3.24 us
    ppermute x1, starting transfers between devices, fast_device(): after = lax.ppermute(low, 'gx', down)  3.14 us
    ppermute x1, starting transfers between devices, fast_device(): before = lax.ppermute(high, 'gx', up)  3.02 us
    ppermute x1, waiting for transfers between devices, fast_device(): after = lax.ppermute(low, 'gx', down)  2.21 us
  transfers between devices with their start and end apart: 6, of which 5 were waited for; matrix products, arithmetic and copies ran while one was open for 0% of the time, Pallas kernels for 17%

profile of v1, /device:TPU:0, one launch (start us, length us, event | category | flops | bytes accessed | tf_op | source)
XLA Modules:
  0.0 75.6 jit_solution(13216276342525468347)
XLA Ops:
  7.2 0.0 all-gather.5.cloned.1.call-start
  7.2 0.0 copy-start.1
  7.2 1.0 %copy-done.1 = f32[3,8,128,32]{2,3,1,0:T(8,128)S(1)} copy-done((f32[3,8,128,32]{2,3,1,0:T(8,128)S(1)}, f32[3,8,128,32]{2,3,1,0:T(8,128)}, u32[]{:S(2)}) %copy-start.1) | copy-done | bytes 393240
  8.2 0.9 %copy-done.3 = f32[8,128,32]{1,2,0:T(8,128)S(1)} copy-done((f32[8,128,32]{1,2,0:T(8,128)S(1)}, f32[8,128,32]{1,2,0:T(8,128)}, u32[]{:S(2)}) %copy-start.3) | copy-done | bytes 131096
  9.1 0.9 %copy-done.5 = f32[8,128,32]{1,2,0:T(8,128)S(1)} copy-done((f32[8,128,32]{1,2,0:T(8,128)S(1)}, f32[8,128,32]{1,2,0:T(8,128)}, u32[]{:S(2)}) %copy-start.5) | copy-done | bytes 131096
  10.0 0.9 %shard_map.86 = (f32[5,8,32,128]{3,2,1,0:T(8,128)}, f32[4,4,32,128]{3,2,1,0:T(8,128)S(1)}, f32[4,4,32,128]{3,2,1,0:T(8,128)S(1)}) custom-call(f32[8,32,128]{2,1,0:T(8,128)S(1)} %bitcast.11, f32[3,8,32,128]{3,2,1,0:T(8,128)S(1)} %bitcast.9, f32[8,32,128]{2,1,0:T(8,128)S(1)} %bitcast.13), custom_call_target="tpu_custom_call" | custom-call | flops 1000000000 | bytes 3333333 | tf_op jit(solution)/shard_map/pallas_call | solution.py:309
  10.9 0.0 all-gather.5.cloned.1.call-update
  11.0 0.0 all-gather.7.cloned.1.call-start
  11.0 3.0 %collective-permute-start = (f32[4,4,32,128]{3,2,1,0:T(8,128)S(1)}, f32[4,4,32,128]{3,2,1,0:T(8,128)S(1)}, u32[]{:S(2)}, u32[]{:S(2)}) collective-permute-start(f32[4,4,32,128]{3,2,1,0:T(8,128)S(1)} %get-tuple-element.16), channel_id=1, source_target_pairs={{0,4},{4,8},{8,12},{12,16},{16,20},{20,24},{24,28},{28,0},{1,5},{5... | collective-permute-start | bytes 786440 | tf_op jit(solution)/shard_map/ppermute | solution.py:341
  14.0 3.1 %collective-permute-start.1 = (f32[4,4,32,128]{3,2,1,0:T(8,128)S(1)}, f32[4,4,32,128]{3,2,1,0:T(8,128)S(1)}, u32[]{:S(2)}, u32[]{:S(2)}) collective-permute-start(f32[4,4,32,128]{3,2,1,0:T(8,128)S(1)} %get-tuple-element.17), channel_id=1, source_target_pairs={{4,0},{8,4},{12,8},{16,12},{20,16},{24,20},{28,24},{0,28},{5,1},{9... | collective-permute-start | bytes 786440 | tf_op jit(solution)/shard_map/ppermute | solution.py:342
  17.2 8.0 %collective-permute-done.before = f32[4,4,32,128]{3,2,1,0:T(8,128)S(1)} collective-permute-done((f32[4,4,32,128]{3,2,1,0:T(8,128)S(1)}, f32[4,4,32,128]{3,2,1,0:T(8,128)S(1)}, u32[]{:S(2)}, u32[]{:S(2)}) %collective-permute-start) | collective-permute-done | bytes 262176 | tf_op jit(solution)/shard_map/ppermute | solution.py:341
  25.2 2.2 %collective-permute-done.1.after = f32[4,4,32,128]{3,2,1,0:T(8,128)S(1)} collective-permute-done((f32[4,4,32,128]{3,2,1,0:T(8,128)S(1)}, f32[4,4,32,128]{3,2,1,0:T(8,128)S(1)}, u32[]{:S(2)}, u32[]{:S(2)}) %collective-permute-start.1) | collective-permute-done | bytes 262176 | tf_op jit(solution)/shard_map/ppermute | solution.py:342
  27.4 0.0 copy-done.10
  27.4 2.7 %shard_map.87 = (f32[4,8,32,128]{3,2,1,0:T(8,128)S(1)}, f32[4,8,32,128]{3,2,1,0:T(8,128)S(1)}, f32[8,32,128]{2,1,0:T(8,128)S(1)}, f32[2,8,32,128]{3,2,1,0:T(8,128)}) custom-call(f32[5,8,32,128]{3,2,1,0:T(8,128)} %get-tuple-element.15.prim, f32[4,4,32,128]{3,2,1,0:T(8,128)S(1)} %collective-permute-done.before, ...), custom_call_target="tpu_custom_call" | custom-call | flops 2000000000 | bytes 6666666 | tf_op jit(solution)/shard_map/pallas_call | solution.py:309
  30.1 0.0 all-gather.7.cloned.1.call-update
  30.1 9.2 %all-gather.5.cloned.1.call-done = f32[20,8,32,128]{3,2,1,0:T(8,128)} async-done(((f32[5,8,32,128]{3,2,1,0:T(8,128)}), f32[20,8,32,128]{3,2,1,0:T(8,128)}) %all-gather.5.cloned.1.call-update) | async-done | bytes 2621456 | tf_op jit(solution)/shard_map/all_gather | solution.py:340
  39.4 3.0 %shard_map.88 = (f32[4,8,32,128]{3,2,1,0:T(8,128)S(1)}, f32[5,8,32,128]{3,2,1,0:T(8,128)S(1)}, f32[5,4,32,128]{3,2,1,0:T(8,128)S(1)}, f32[5,4,32,128]{3,2,1,0:T(8,128)S(1)}) custom-call(s32[1]{0:T(128)} %bitcast.me, f32[5,8,32,128]{3,2,1,0:T(8,128)} %get-tuple-element.15.prim, f32[4,5,8,32,128]{4,3,2,1,0:T(8,128)} %bitcast.15, ...), custom_call_target="tpu_custom_call" | custom-call | flops 2000000000 | bytes 6666666 | tf_op jit(solution)/shard_map/pallas_call | solution.py:309
  42.4 0.0 copy-start.11
  42.5 0.8 %copy-done.11 = f32[5,8,32,128]{3,2,1,0:T(8,128)} copy-done((f32[5,8,32,128]{3,2,1,0:T(8,128)}, f32[5,8,32,128]{3,2,1,0:T(8,128)S(1)}, u32[]{:S(2)}) %copy-start.11) | copy-done | bytes 655384
  43.3 1.5 %collective-permute-start.2 = (f32[5,4,32,128]{3,2,1,0:T(8,128)S(1)}, f32[5,4,32,128]{3,2,1,0:T(8,128)S(1)}, u32[]{:S(2)}, u32[]{:S(2)}) collective-permute-start(f32[5,4,32,128]{3,2,1,0:T(8,128)S(1)} %get-tuple-element.24), channel_id=1, source_target_pairs={{0,4},{4,8},{8,12},{12,16},{16,20},{20,24},{24,28},{28,0},{1,5},{5... | collective-permute-start | bytes 983048 | tf_op jit(solution)/shard_map/ppermute | solution.py:352
  44.8 3.2 %collective-permute-start.3 = (f32[5,4,32,128]{3,2,1,0:T(8,128)S(1)}, f32[5,4,32,128]{3,2,1,0:T(8,128)S(1)}, u32[]{:S(2)}, u32[]{:S(2)}) collective-permute-start(f32[5,4,32,128]{3,2,1,0:T(8,128)S(1)} %get-tuple-element.25), channel_id=1, source_target_pairs={{4,0},{8,4},{12,8},{16,12},{20,16},{24,20},{28,24},{0,28},{5,1},{9... | collective-permute-start | bytes 983048 | tf_op jit(solution)/shard_map/ppermute | solution.py:353
  48.0 1.1 %copy-done.16 = f32[4,8,32,128]{3,2,1,0:T(8,128)S(1)} copy-done((f32[4,8,32,128]{3,2,1,0:T(8,128)S(1)}, f32[4,8,32,128]{3,2,1,0:T(8,128)}, u32[]{:S(2)}) %copy-start.16) | copy-done | bytes 524312
  49.1 1.0 %copy-done.18 = f32[4,8,32,128]{3,2,1,0:T(8,128)S(1)} copy-done((f32[4,8,32,128]{3,2,1,0:T(8,128)S(1)}, f32[4,8,32,128]{3,2,1,0:T(8,128)}, u32[]{:S(2)}) %copy-start.18) | copy-done | bytes 524312
  50.1 6.9 %shard_map.89.part = f32[5,8,32,128]{3,2,1,0:T(8,128)S(1)} custom-call(s32[1]{0:T(128)} %bitcast.me, f32[5,8,32,128]{3,2,1,0:T(8,128)} %get-tuple-element.15.prim, f32[4,5,8,32,128]{4,3,2,1,0:T(8,128)} %bitcast.16, f32[4,8,32,128]{3,2,1,0:T(8,128)S(1)} %copy-done.16, f32[4,8,32,128]{3,2,1,0:T(8,128)S(1)} %copy-done.18, ...), custom_call_target="tpu_custom_call" | custom-call | flops 4000000000 | bytes 13333333 | tf_op jit(solution)/shard_map/pallas_call | solution.py:309
  57.1 0.0 copy-start.13
  57.1 0.8 %copy-done.13 = f32[5,8,32,128]{3,2,1,0:T(8,128)} copy-done((f32[5,8,32,128]{3,2,1,0:T(8,128)}, f32[5,8,32,128]{3,2,1,0:T(8,128)S(1)}, u32[]{:S(2)}) %copy-start.13) | copy-done | bytes 655384
  57.9 1.2 %collective-permute-done.2.before = f32[5,4,32,128]{3,2,1,0:T(8,128)S(1)} collective-permute-done((f32[5,4,32,128]{3,2,1,0:T(8,128)S(1)}, f32[5,4,32,128]{3,2,1,0:T(8,128)S(1)}, u32[]{:S(2)}, u32[]{:S(2)}) %collective-permute-start.2) | collective-permute-done | bytes 327712 | tf_op jit(solution)/shard_map/ppermute | solution.py:352
  59.2 2.2 %collective-permute-done.3.after = f32[5,4,32,128]{3,2,1,0:T(8,128)S(1)} collective-permute-done((f32[5,4,32,128]{3,2,1,0:T(8,128)S(1)}, f32[5,4,32,128]{3,2,1,0:T(8,128)S(1)}, u32[]{:S(2)}, u32[]{:S(2)}) %collective-permute-start.3) | collective-permute-done | bytes 327712 | tf_op jit(solution)/shard_map/ppermute | solution.py:353
  61.4 1.2 %copy-done = f32[8,8,32,128]{3,2,1,0:T(8,128)S(1)} copy-done((f32[8,8,32,128]{3,2,1,0:T(8,128)S(1)}, f32[8,8,32,128]{3,2,1,0:T(8,128)}, u32[]{:S(2)}) %copy-start) | copy-done | bytes 1048600
  62.6 1.1 %copy-done.12 = f32[5,8,32,128]{3,2,1,0:T(8,128)S(1)} copy-done((f32[5,8,32,128]{3,2,1,0:T(8,128)S(1)}, f32[5,8,32,128]{3,2,1,0:T(8,128)}, u32[]{:S(2)}) %copy-start.12) | copy-done | bytes 655384
  63.7 1.1 %copy-done.14 = f32[5,8,32,128]{3,2,1,0:T(8,128)S(1)} copy-done((f32[5,8,32,128]{3,2,1,0:T(8,128)S(1)}, f32[5,8,32,128]{3,2,1,0:T(8,128)}, u32[]{:S(2)}) %copy-start.14) | copy-done | bytes 655384
  64.8 4.0 %shard_map.90 = (f32[5,8,32,128]{3,2,1,0:T(8,128)}, f32[5,8,32,128]{3,2,1,0:T(8,128)}) custom-call(s32[1]{0:T(128)} %bitcast.me, f32[8,32,128]{2,1,0:T(8,128)S(1)} %bitcast.12, f32[3,8,32,128]{3,2,1,0:T(8,128)S(1)} %bitcast.10, f32[8,32,128]{2,1,0:T(8,128)S(1)} %bitcast.14, f32[4,5,8,32,128]{4,3,2,1,0:T(8,128)} %bitcast.17, ...), custom_call_target="tpu_custom_call" | custom-call | flops 2000000000 | bytes 6666666 | tf_op jit(solution)/shard_map/pallas_call | solution.py:309
  (25 shorter events, 0.0 us)
Async XLA Ops:
  7.2 32.2 %all-gather.5.cloned.1.call-start = ((), (), s32[]{:S(2)}) async-start(), calls=%async_computation | async-start | bytes 3276800 | tf_op jit(solution)/shard_map/all_gather | solution.py:340
  7.2 1.0 %copy-start.1 = (f32[3,8,128,32]{2,3,1,0:T(8,128)S(1)}, f32[3,8,128,32]{2,3,1,0:T(8,128)}, u32[]{:S(2)}) copy-start(f32[3,8,128,32]{2,3,1,0:T(8,128)} %param.8) | copy-start | bytes 1179652
  8.2 0.9 %copy-start.3 = (f32[8,128,32]{1,2,0:T(8,128)S(1)}, f32[8,128,32]{1,2,0:T(8,128)}, u32[]{:S(2)}) copy-start(f32[8,128,32]{1,2,0:T(8,128)} %param.7) | copy-start | bytes 393220
  9.1 0.9 %copy-start.5 = (f32[8,128,32]{1,2,0:T(8,128)S(1)}, f32[8,128,32]{1,2,0:T(8,128)}, u32[]{:S(2)}) copy-start(f32[8,128,32]{1,2,0:T(8,128)} %param.9) | copy-start | bytes 393220
  10.0 17.4 %copy-start.9 = (bf16[256,256]{1,0:T(8,128)(2,1)S(1)}, bf16[256,256]{1,0:T(8,128)(2,1)}, u32[]{:S(2)}) copy-start(bf16[256,256]{1,0:T(8,128)(2,1)} %constant.14.clone.y_high) | copy-start | bytes 393220
  10.0 17.4 %copy-start.10 = (bf16[256,256]{1,0:T(8,128)(2,1)S(1)}, bf16[256,256]{1,0:T(8,128)(2,1)}, u32[]{:S(2)}) copy-start(bf16[256,256]{1,0:T(8,128)(2,1)} %constant.15.clone.y_low) | copy-start | bytes 393220
  11.0 47.0 %all-gather.7.cloned.1.call-start = ((), (), s32[]{:S(2)}) async-start(), calls=%async_computation.1 | async-start | bytes 1310720 | tf_op jit(solution)/shard_map/all_gather | solution.py:347
  11.0 14.2 %collective-permute-start = (f32[4,4,32,128]{3,2,1,0:T(8,128)S(1)}, f32[4,4,32,128]{3,2,1,0:T(8,128)S(1)}, u32[]{:S(2)}, u32[]{:S(2)}) collective-permute-start(f32[4,4,32,128]{3,2,1,0:T(8,128)S(1)} %get-tuple-element.16), channel_id=1, source_target_pairs={{0,4},{4,8},{8,12},{12,16},{16,20},{20,24},{24,28},{28,0},{1,5},{5... | collective-permute-start | bytes 786440 | tf_op jit(solution)/shard_map/ppermute | solution.py:341
  14.0 25.3 %copy-start.7 = (bf16[512,512]{1,0:T(8,128)(2,1)S(1)}, bf16[512,512]{1,0:T(8,128)(2,1)}, u32[]{:S(2)}) copy-start(bf16[512,512]{1,0:T(8,128)(2,1)} %constant.12.clone.z_high) | copy-start | bytes 1572868
  14.0 25.3 %copy-start.8 = (bf16[512,512]{1,0:T(8,128)(2,1)S(1)}, bf16[512,512]{1,0:T(8,128)(2,1)}, u32[]{:S(2)}) copy-start(bf16[512,512]{1,0:T(8,128)(2,1)} %constant.13.clone.z_low) | copy-start | bytes 1572868
  14.0 13.4 %collective-permute-start.1 = (f32[4,4,32,128]{3,2,1,0:T(8,128)S(1)}, f32[4,4,32,128]{3,2,1,0:T(8,128)S(1)}, u32[]{:S(2)}, u32[]{:S(2)}) collective-permute-start(f32[4,4,32,128]{3,2,1,0:T(8,128)S(1)} %get-tuple-element.17), channel_id=1, source_target_pairs={{4,0},{8,4},{12,8},{16,12},{20,16},{24,20},{28,24},{0,28},{5,1},{9... | collective-permute-start | bytes 786440 | tf_op jit(solution)/shard_map/ppermute | solution.py:342
  30.1 12.3 %copy-start.15 = (f32[4,8,32,128]{3,2,1,0:T(8,128)}, f32[4,8,32,128]{3,2,1,0:T(8,128)S(1)}, u32[]{:S(2)}) copy-start(f32[4,8,32,128]{3,2,1,0:T(8,128)S(1)} %get-tuple-element.19.dx) | copy-start | bytes 1572868
  30.1 12.3 %copy-start.17 = (f32[4,8,32,128]{3,2,1,0:T(8,128)}, f32[4,8,32,128]{3,2,1,0:T(8,128)S(1)}, u32[]{:S(2)}) copy-start(f32[4,8,32,128]{3,2,1,0:T(8,128)S(1)} %get-tuple-element.20.dy) | copy-start | bytes 1572868
  42.4 0.8 %copy-start.11 = (f32[5,8,32,128]{3,2,1,0:T(8,128)}, f32[5,8,32,128]{3,2,1,0:T(8,128)S(1)}, u32[]{:S(2)}) copy-start(f32[5,8,32,128]{3,2,1,0:T(8,128)S(1)} %get-tuple-element.23.flux) | copy-start | bytes 1966084
  43.3 15.9 %collective-permute-start.2 = (f32[5,4,32,128]{3,2,1,0:T(8,128)S(1)}, f32[5,4,32,128]{3,2,1,0:T(8,128)S(1)}, u32[]{:S(2)}, u32[]{:S(2)}) collective-permute-start(f32[5,4,32,128]{3,2,1,0:T(8,128)S(1)} %get-tuple-element.24), channel_id=1, source_target_pairs={{0,4},{4,8},{8,12},{12,16},{16,20},{20,24},{24,28},{28,0},{1,5},{5... | collective-permute-start | bytes 983048 | tf_op jit(solution)/shard_map/ppermute | solution.py:352
  44.8 16.6 %collective-permute-start.3 = (f32[5,4,32,128]{3,2,1,0:T(8,128)S(1)}, f32[5,4,32,128]{3,2,1,0:T(8,128)S(1)}, u32[]{:S(2)}, u32[]{:S(2)}) collective-permute-start(f32[5,4,32,128]{3,2,1,0:T(8,128)S(1)} %get-tuple-element.25), channel_id=1, source_target_pairs={{4,0},{8,4},{12,8},{16,12},{20,16},{24,20},{28,24},{0,28},{5,1},{9... | collective-permute-start | bytes 983048 | tf_op jit(solution)/shard_map/ppermute | solution.py:353
  48.0 1.1 %copy-start.16 = (f32[4,8,32,128]{3,2,1,0:T(8,128)S(1)}, f32[4,8,32,128]{3,2,1,0:T(8,128)}, u32[]{:S(2)}) copy-start(f32[4,8,32,128]{3,2,1,0:T(8,128)} %copy-done.15) | copy-start | bytes 1572868
  49.1 1.0 %copy-start.18 = (f32[4,8,32,128]{3,2,1,0:T(8,128)S(1)}, f32[4,8,32,128]{3,2,1,0:T(8,128)}, u32[]{:S(2)}) copy-start(f32[4,8,32,128]{3,2,1,0:T(8,128)} %copy-done.17) | copy-start | bytes 1572868
  50.1 11.2 %copy-start.2 = (f32[3,8,128,32]{2,3,1,0:T(8,128)S(1)}, f32[3,8,128,32]{2,3,1,0:T(8,128)}, u32[]{:S(2)}) copy-start(f32[3,8,128,32]{2,3,1,0:T(8,128)} %param.8) | copy-start | bytes 1179652
  50.1 11.2 %copy-start.4 = (f32[8,128,32]{1,2,0:T(8,128)S(1)}, f32[8,128,32]{1,2,0:T(8,128)}, u32[]{:S(2)}) copy-start(f32[8,128,32]{1,2,0:T(8,128)} %param.7) | copy-start | bytes 393220
  50.1 11.2 %copy-start.6 = (f32[8,128,32]{1,2,0:T(8,128)S(1)}, f32[8,128,32]{1,2,0:T(8,128)}, u32[]{:S(2)}) copy-start(f32[8,128,32]{1,2,0:T(8,128)} %param.9) | copy-start | bytes 393220
  57.1 0.8 %copy-start.13 = (f32[5,8,32,128]{3,2,1,0:T(8,128)}, f32[5,8,32,128]{3,2,1,0:T(8,128)S(1)}, u32[]{:S(2)}) copy-start(f32[5,8,32,128]{3,2,1,0:T(8,128)S(1)} %shard_map.89.part) | copy-start | bytes 1966084
  61.4 1.2 %copy-start = (f32[8,8,32,128]{3,2,1,0:T(8,128)S(1)}, f32[8,8,32,128]{3,2,1,0:T(8,128)}, u32[]{:S(2)}) copy-start(f32[8,8,32,128]{3,2,1,0:T(8,128)} %all-gather.7.cloned.1.call-done) | copy-start | bytes 3145732
  62.6 1.1 %copy-start.12 = (f32[5,8,32,128]{3,2,1,0:T(8,128)S(1)}, f32[5,8,32,128]{3,2,1,0:T(8,128)}, u32[]{:S(2)}) copy-start(f32[5,8,32,128]{3,2,1,0:T(8,128)} %copy-done.11) | copy-start | bytes 1966084
  63.7 1.1 %copy-start.14 = (f32[5,8,32,128]{3,2,1,0:T(8,128)S(1)}, f32[5,8,32,128]{3,2,1,0:T(8,128)}, u32[]{:S(2)}) copy-start(f32[5,8,32,128]{3,2,1,0:T(8,128)} %copy-done.13) | copy-start | bytes 1966084
Sparse Core Ops, SparseCore 0:
  11.1 28.2 all-gather.4
  40.9 16.7 all-gather.6
